TPU v7x, 256 devices: a whole 4x4x8 slice. The times are simulated.
256 devices in a mesh: row: 16 (over z, core), col: 4 (over y), rep: 4 (over x).
Axes of the slice: x: 4, y: 4, z: 8, core: 2. Of those that a mesh axis runs over, the one named last changes fastest.
Arguments:
- density: bfloat16 [8192, 8192], P('row', 'col'), may hold values from -1.5 to 1.75, as said below
- pattern_density: int32 [256, 256], P('row', 'col'), may hold values 0 or 1
- pattern_square: int32 [256, 256], P('row', 'col'), may hold values 0 or 1
- pattern_cube: int32 [256, 256], P('row', 'col'), may hold values 0 or 1
Outputs:
- purified: bfloat16 [8192, 8192], P('row', ('col', 'rep'))
Inputs may be any that keep to these rules, and one draw needn't show every extreme that they name: `density`: symmetric.
All inputs are finite; a program needn't handle non-finite values. No bound on the sum of `pattern_density` or of `pattern_square` or of `pattern_cube` on one device may be relied on, other than what follows from the above.
Results may differ from a plain program's by a relative error of at most 0.0054.
Values may be sent and summed in bfloat16 or wider, within the bound.
No kernel may reach another device: no remote copies, remote signals or barrier semaphores. Data moves between devices by JAX's collectives and lax.ppermute only.
A program may use at most 64 MiB of HBM per device.

v0:
```python
import jax
import jax.numpy as jnp
from jax import lax
from jax.sharding import PartitionSpec as P

BLK = 32


def spread(pattern, block_width):
    blocks_down, blocks_across = pattern.shape
    wide = jnp.broadcast_to(
        pattern[:, None, :, None] > 0, (blocks_down, block_width, blocks_across, block_width)
    )
    return wide.reshape(blocks_down * block_width, blocks_across * block_width)


def column_share(matrix, rep_depth, rep_layer, block_width):
    tile_rows, tile_width = matrix.shape
    shaped = matrix.reshape(
        tile_rows, tile_width // (rep_depth * block_width), rep_depth, block_width
    )
    picked = lax.dynamic_index_in_dim(shaped, rep_layer, 2, keepdims=False)
    return picked.reshape(tile_rows, tile_width // rep_depth)


def row_share(matrix, rep_depth, rep_layer, block_width):
    tile_rows, tile_width = matrix.shape
    shaped = matrix.reshape(
        tile_rows // (rep_depth * block_width), rep_depth, block_width, tile_width
    )
    picked = lax.dynamic_index_in_dim(shaped, rep_layer, 1, keepdims=False)
    return picked.reshape(tile_rows // rep_depth, tile_width)


def body(density, pattern_density, pattern_square, pattern_cube):
    tile_rows, tile_width = density.shape
    rep_depth = lax.axis_size("rep")
    rep_layer = lax.axis_index("rep")
    share_width = tile_width // rep_depth
    share_start = rep_layer * share_width
    masked = jnp.where(spread(pattern_density, BLK), density, jnp.zeros_like(density))
    right_share = row_share(masked, rep_depth, rep_layer, BLK)
    left_band = lax.all_gather(
        column_share(masked, rep_depth, rep_layer, BLK), "col", axis=1, tiled=True
    )
    right_band = lax.all_gather(right_share, "row", axis=0, tiled=True)
    product_one = jnp.dot(left_band, right_band, preferred_element_type=jnp.float32)
    square_keep = spread(pattern_square, BLK)
    summed = lax.psum(product_one, "rep")
    square = jnp.where(square_keep, summed, jnp.float32(0.0)).astype(jnp.bfloat16)
    left_square = lax.all_gather(
        column_share(square, rep_depth, rep_layer, BLK), "col", axis=1, tiled=True
    )
    product_two = jnp.dot(left_square, right_band, preferred_element_type=jnp.float32)
    cube_share = lax.psum_scatter(product_two, "rep", scatter_dimension=1, tiled=True)
    cube_keep = lax.dynamic_slice_in_dim(spread(pattern_cube, BLK), share_start, share_width, 1)
    square_cols = lax.dynamic_slice_in_dim(square, share_start, share_width, 1).astype(jnp.float32)
    cube = jnp.where(cube_keep, cube_share, jnp.float32(0.0))
    return (3.0 * square_cols - 2.0 * cube).astype(jnp.bfloat16)


def solution(mesh):
    placed = (P("row", "col"), P("row", "col"), P("row", "col"), P("row", "col"))
    return jax.shard_map(
        body, mesh=mesh, in_specs=placed, out_specs=P("row", ("col", "rep")), check_vma=False
    )
```

profile of v0, /device:TPU:1, one launch (start us, length us, event | category | flops | bytes accessed | tf_op | source)
XLA Modules:
  0.0 318.8 jit_solution(17400307454804896158)
XLA Ops:
  6.5 0.0 all-gather.4.cloned.1.call-start
  6.5 0.7 broadcast_compare_fusion.1
  7.2 3.1 broadcast_in_dim.30
  10.3 10.4 %reshape.37 = pred[512,2048]{1,0:T(8,128)(4,1)S(1)} reshape(pred[16,32,64,32]{3,2,1,0:T(8,128)(4,1)} %broadcast_in_dim.30) | data formatting | bytes 2097152 | tf_op jit(solution)/shard_map/reshape | solution.py:14
  20.7 1.8 broadcast_select_fusion
  22.5 2.5 copy.5
  25.0 0.0 copy-start
  25.0 1.9 constant_dynamic-slice_fusion.2
  26.9 0.0 all-gather.4.cloned.1.call-update
  27.0 0.0 all-gather.6.cloned.1.call-start
  27.0 0.9 constant_dynamic-slice_fusion.1
  27.9 0.0 all-gather.6.cloned.1.call-update
  27.9 0.0 all-gather.8.cloned.1.call-start
  27.9 0.0 copy-done
  28.0 3.1 broadcast_in_dim.15
  31.1 10.4 %reshape.36 = pred[512,2048]{1,0:T(8,128)(4,1)S(1)} reshape(pred[16,32,64,32]{3,2,1,0:T(8,128)(4,1)} %broadcast_in_dim.15) | data formatting | bytes 2097152 | tf_op jit(solution)/shard_map/reshape | solution.py:14
  41.4 22.9 %all-gather.4.cloned.1.call-done = bf16[512,2048]{0,1:T(8,128)(2,1)} async-done(((bf16[512,512]{0,1:T(8,128)(2,1)}), bf16[512,2048]{0,1:T(8,128)(2,1)}) %all-gather.4.cloned.1.call-update) | async-done | bytes 2097168 | tf_op jit(solution)/shard_map/all_gather | solution.py:43
  64.3 58.2 %all-gather.6.cloned.1.call-done = bf16[2048,2048]{1,0:T(8,128)(2,1)} async-done(((bf16[128,2048]{1,0:T(8,128)(2,1)}), bf16[2048,2048]{1,0:T(8,128)(2,1)}) %all-gather.6.cloned.1.call-update) | async-done | bytes 8388624 | tf_op jit(solution)/shard_map/all_gather | solution.py:46
  122.5 10.5 %fusion = f32[512,2048]{1,0:T(8,128)} fusion(bf16[512,2048]{0,1:T(8,128)(2,1)} %all-gather.4.cloned.1.call-done, bf16[2048,2048]{1,0:T(8,128)(2,1)} %all-gather.6.cloned.1.call-done), kind=kOutput, calls=%fused_computation.9 | convolution fusion | flops 4294967296 | bytes 14680064 | tf_op jit(solution)/shard_map/dot_general | solution.py:47
  133.1 78.3 %all-reduce.1 = bf16[512,2048]{1,0:T(8,128)(2,1)} all-reduce(f32[512,2048]{1,0:T(8,128)} %fusion), channel_id=1, replica_groups=mesh['row'=16,'col'=4,'rep'=4] {'rep'}, use_global_device_ids=true, to_apply=%region_0.1 | all-reduce | flops 1048576 | bytes 6291456 | tf_op jit(solution)/shard_map/psum | solution.py:49
  211.4 2.3 select_convert_fusion
  213.7 2.6 copy.6
  216.3 1.9 constant_dynamic-slice_fusion
  218.1 0.0 all-gather.8.cloned.1.call-update
  218.2 0.2 reduce-scatter.2.cloned.1.call-start
  218.4 31.4 %all-gather.8.cloned.1.call-done = bf16[512,2048]{0,1:T(8,128)(2,1)} async-done(((bf16[512,512]{0,1:T(8,128)(2,1)}), bf16[512,2048]{0,1:T(8,128)(2,1)}) %all-gather.8.cloned.1.call-update) | async-done | bytes 2097168 | tf_op jit(solution)/shard_map/all_gather | solution.py:51
  249.8 10.5 %fusion.1 = f32[512,2048]{1,0:T(8,128)} fusion(bf16[512,2048]{0,1:T(8,128)(2,1)} %all-gather.8.cloned.1.call-done, bf16[2048,2048]{1,0:T(8,128)(2,1)} %all-gather.6.cloned.1.call-done), kind=kOutput, calls=%fused_computation.10 | convolution fusion | flops 4294967296 | bytes 14680064 | tf_op jit(solution)/shard_map/dot_general | solution.py:54
  260.3 0.0 copy-start.1
  260.3 0.0 reduce-scatter.2.cloned.1.call-update
  260.3 0.7 copy-done.1
  261.0 3.1 broadcast_in_dim.33
  264.1 10.5 %reshape.42 = pred[512,2048]{1,0:T(8,128)(4,1)S(1)} reshape(pred[16,32,64,32]{3,2,1,0:T(8,128)(4,1)} %broadcast_in_dim.33) | data formatting | bytes 2097152 | tf_op jit(solution)/shard_map/reshape | solution.py:14
  274.6 35.3 %reduce-scatter.2.cloned.1.call-done = f32[512,512]{1,0:T(8,128)} async-done(((f32[512,2048]{1,0:T(8,128)}), f32[512,512]{1,0:T(8,128)}) %reduce-scatter.2.cloned.1.call-update) | async-done | bytes 1048592 | tf_op jit(solution)/shard_map/reduce_scatter | solution.py:55
  309.9 2.3 subtract_convert_fusion
  (2 shorter events, 0.0 us)
Async XLA Ops:
  6.5 57.8 %all-gather.4.cloned.1.call-start = ((), (), s32[]{:S(2)}) async-start(), calls=%async_computation.1 | async-start | bytes 2621440 | tf_op jit(solution)/shard_map/all_gather | solution.py:43
  25.0 2.9 copy-start
  27.0 95.6 %all-gather.6.cloned.1.call-start = ((), (), s32[]{:S(2)}) async-start(), calls=%async_computation.2 | async-start | bytes 8912896 | tf_op jit(solution)/shard_map/all_gather | solution.py:46
  27.9 221.9 %all-gather.8.cloned.1.call-start = ((), (), s32[]{:S(2)}) async-start(), calls=%async_computation.3 | async-start | bytes 2621440 | tf_op jit(solution)/shard_map/all_gather | solution.py:51
  218.2 91.7 %reduce-scatter.2.cloned.1.call-start = ((), (), s32[]{:S(2)}) async-start(), calls=%async_computation.4 | async-start | bytes 5242880 | tf_op jit(solution)/shard_map/reduce_scatter | solution.py:55
  260.3 0.7 copy-start.1
Sparse Core Ops, SparseCore 0:
  27.1 37.2 all-gather.3
  66.1 56.3 all-gather.5
  218.3 31.4 all-gather.7
  260.5 49.4 reduce-scatter.1
where the time goes:
time: 320 us; the launch traced here: 319 us
  waiting for transfers between devices  148 us (46%)
  blocking collectives  78.3 us (24%)
  local copies, waits for them, and re-layouts  50.9 us (16%)
  matrix products  21.1 us (7%)
  between operations  13.2 us (4%)
  other arithmetic  7.09 us (2%)
    psum x1, blocking collectives, body(): summed = lax.psum(product_one, 'rep')  78.3 us
    all_gather x1, waiting for transfers between devices, body(): right_band = lax.all_gather(right_share, 'row', axis=0, tiled=True)  58.2 us
    reduce_scatter x1, waiting for transfers between devices, body(): lax.psum_scatter(product_two, 'rep', scatter_dimension=1, tiled=True)  35.3 us
    all_gather x1, waiting for transfers between devices, body(): lax.all_gather(column_share(square, rep_depth, rep_layer, BLK), 'col', ax...  31.4 us
    reshape x3, local copies, waits for them, and re-layouts, spread(): return wide.reshape(blocks_down * block_width, blocks_across * block_width)  31.3 us
    all_gather x1, waiting for transfers between devices, body(): lax.all_gather(column_share(masked, rep_depth, rep_layer, BLK), 'col', ax...  22.9 us
    dot_general x1, matrix products, body(): jnp.dot(left_square, right_band, preferred_element_type=jnp.float32)  10.5 us
    dot_general x1, matrix products, body(): jnp.dot(left_band, right_band, preferred_element_type=jnp.float32)  10.5 us
  transfers between devices with their start and end apart: 4, of which 4 were waited for; matrix products, arithmetic and copies ran while one was open for 9% of the time, Pallas kernels for 0%

commit v1 on v0

--- a/solution.py
+++ b/solution.py
@@ -1,9 +1,23 @@
+import functools
 import jax
 import jax.numpy as jnp
 from jax import lax
 from jax.sharding import PartitionSpec as P
 
 BLK = 32
+
+
+def raise_heaps_for(view, ax_name):
+    n_all = lax.psum(1, ax_name)
+    response, w2 = (view, 0)
+    while 1 << w2 < n_all:
+        tile_out = lax.ppermute(response, ax_name, [(q, q ^ 1 << w2) for q in range(n_all)])
+        response = response + tile_out
+        w2 = w2 + 1
+    return response
+
+
+pair_fields = functools.partial(raise_heaps_for, ax_name="rep")
 
 
 def spread(pattern, block_width):
@@ -46,7 +60,7 @@
     right_band = lax.all_gather(right_share, "row", axis=0, tiled=True)
     product_one = jnp.dot(left_band, right_band, preferred_element_type=jnp.float32)
     square_keep = spread(pattern_square, BLK)
-    summed = lax.psum(product_one, "rep")
+    summed = pair_fields(product_one)
     square = jnp.where(square_keep, summed, jnp.float32(0.0)).astype(jnp.bfloat16)
     left_square = lax.all_gather(
         column_share(square, rep_depth, rep_layer, BLK), "col", axis=1, tiled=True

time: 320 us -> 431 us (1.35)
  waiting for transfers between devices: 148 us -> 331 us
  blocking collectives: 78.3 us -> 0 us
  other arithmetic: 7.09 us -> 12.3 us
    ppermute x0 -> x2, waiting for transfers between devices: none -> 167 us  [raise_heaps_for(): lax.ppermute(response, ax_name, [(q, q ^ 1 << w2) for q in range(n_all)])]
    psum x1 -> x0, blocking collectives: 78.3 us -> none  [body(): summed = lax.psum(product_one, 'rep')]
    all_gather x1, waiting for transfers between devices: 22.9 us -> 36.4 us  [body(): lax.all_gather(column_share(masked, rep_depth, rep_layer, BLK), 'col', ax...]
  transfers between devices with their start and end apart: 4 -> 6, of which waited for: 4 -> 6; matrix products, arithmetic and copies ran while one was open for 9% -> 7% of each run, Pallas kernels for 0% -> 0%
where the time goes in v1:
time: 431 us; the launch traced here: 429 us
  waiting for transfers between devices  331 us (77%)
  local copies, waits for them, and re-layouts  51 us (12%)
  matrix products  18.1 us (4%)
  between operations  13.2 us (3%)
  other arithmetic  12.3 us (3%)
    ppermute x2, waiting for transfers between devices, raise_heaps_for(): lax.ppermute(response, ax_name, [(q, q ^ 1 << w2) for q in range(n_all)])  167 us
    all_gather x1, waiting for transfers between devices, body(): right_band = lax.all_gather(right_share, 'row', axis=0, tiled=True)  58.2 us
    all_gather x1, waiting for transfers between devices, body(): lax.all_gather(column_share(masked, rep_depth, rep_layer, BLK), 'col', ax...  36.4 us
    reduce_scatter x1, waiting for transfers between devices, body(): lax.psum_scatter(product_two, 'rep', scatter_dimension=1, tiled=True)  35.3 us
    all_gather x1, waiting for transfers between devices, body(): lax.all_gather(column_share(square, rep_depth, rep_layer, BLK), 'col', ax...  33.2 us
    reshape x3, local copies, waits for them, and re-layouts, spread(): return wide.reshape(blocks_down * block_width, blocks_across * block_width)  31.3 us
    dot_general x1, matrix products, body(): jnp.dot(left_square, right_band, preferred_element_type=jnp.float32)  10.6 us
    broadcast_in_dim x3, local copies, waits for them, and re-layouts, spread(): jnp.broadcast_to(pattern[:, None, :, None] > 0, (blocks_down, block_width...  9.29 us
  transfers between devices with their start and end apart: 6, of which 6 were waited for; matrix products, arithmetic and copies ran while one was open for 7% of the time, Pallas kernels for 0%

profile of v1, /device:TPU:1, one launch (start us, length us, event | category | flops | bytes accessed | tf_op | source)
XLA Modules:
  0.0 429.4 jit_solution(4754047633265827870)
XLA Ops:
  6.5 0.0 all-gather.4.cloned.1.call-start
  6.5 0.7 broadcast_compare_fusion.1
  7.2 3.1 broadcast_in_dim.30
  10.3 10.4 %reshape.37 = pred[512,2048]{1,0:T(8,128)(4,1)S(1)} reshape(pred[16,32,64,32]{3,2,1,0:T(8,128)(4,1)} %broadcast_in_dim.30) | data formatting | bytes 2097152 | tf_op jit(solution)/shard_map/reshape | solution.py:28
  20.7 1.8 broadcast_select_fusion
  22.5 2.5 copy.5
  25.1 1.9 constant_dynamic-slice_fusion.2
  26.9 0.0 all-gather.4.cloned.1.call-update
  27.0 0.0 all-gather.6.cloned.1.call-start
  27.0 0.8 constant_dynamic-slice_fusion.1
  27.9 0.0 all-gather.6.cloned.1.call-update
  27.9 0.0 all-gather.8.cloned.1.call-start
  27.9 36.4 %all-gather.4.cloned.1.call-done = bf16[512,2048]{0,1:T(8,128)(2,1)} async-done(((bf16[512,512]{0,1:T(8,128)(2,1)}), bf16[512,2048]{0,1:T(8,128)(2,1)}) %all-gather.4.cloned.1.call-update) | async-done | bytes 2097168 | tf_op jit(solution)/shard_map/all_gather | solution.py:57
  64.3 58.2 %all-gather.6.cloned.1.call-done = bf16[2048,2048]{1,0:T(8,128)(2,1)} async-done(((bf16[128,2048]{1,0:T(8,128)(2,1)}), bf16[2048,2048]{1,0:T(8,128)(2,1)}) %all-gather.6.cloned.1.call-update) | async-done | bytes 8388624 | tf_op jit(solution)/shard_map/all_gather | solution.py:60
  122.6 7.6 %fusion = f32[512,2048]{1,0:T(8,128)S(1)} fusion(bf16[512,2048]{0,1:T(8,128)(2,1)} %all-gather.4.cloned.1.call-done, bf16[2048,2048]{1,0:T(8,128)(2,1)} %all-gather.6.cloned.1.call-done), kind=kOutput, calls=%fused_computation.9 | convolution fusion | flops 4294967296 | bytes 14680064 | tf_op jit(solution)/shard_map/dot_general | solution.py:61
  130.2 0.0 copy-start
  130.2 1.3 collective-permute-start
  131.4 90.7 %collective-permute-done = f32[512,2048]{1,0:T(8,128)S(1)} collective-permute-done((f32[512,2048]{1,0:T(8,128)S(1)}, f32[512,2048]{1,0:T(8,128)S(1)}, u32[]{:S(2)}, u32[]{:S(2)}) %collective-permute-start) | collective-permute-done | bytes 4194336 | tf_op jit(solution)/shard_map/ppermute | solution.py:14
  222.2 2.7 add.20
  224.9 2.7 collective-permute-start.1
  227.6 0.0 copy-done
  227.6 3.1 broadcast_in_dim.15
  230.7 10.4 %reshape.36 = pred[512,2048]{1,0:T(8,128)(4,1)S(1)} reshape(pred[16,32,64,32]{3,2,1,0:T(8,128)(4,1)} %broadcast_in_dim.15) | data formatting | bytes 2097152 | tf_op jit(solution)/shard_map/reshape | solution.py:28
  241.1 76.6 %collective-permute-done.1 = f32[512,2048]{1,0:T(8,128)} collective-permute-done((f32[512,2048]{1,0:T(8,128)}, f32[512,2048]{1,0:T(8,128)}, u32[]{:S(2)}, u32[]{:S(2)}) %collective-permute-start.1) | collective-permute-done | bytes 4194336 | tf_op jit(solution)/shard_map/ppermute | solution.py:14
  317.7 4.7 %select_convert_fusion = bf16[512,2048]{1,0:T(8,128)(2,1)S(1)} fusion(pred[512,2048]{1,0:T(8,128)(4,1)S(1)} %reshape.36, f32[512,2048]{1,0:T(8,128)} %add.20, f32[512,2048]{1,0:T(8,128)} %collective-permute-done.1), kind=kLoop, calls=%fused_computation | loop fusion | flops 3145728 | bytes 11534336 | tf_op jit(solution)/shard_map/convert_element_type | solution.py:64
  322.4 2.6 copy.6
  325.0 1.9 constant_dynamic-slice_fusion
  326.9 0.0 all-gather.8.cloned.1.call-update
  326.9 0.2 reduce-scatter.2.cloned.1.call-start
  327.2 33.2 %all-gather.8.cloned.1.call-done = bf16[512,2048]{0,1:T(8,128)(2,1)} async-done(((bf16[512,512]{0,1:T(8,128)(2,1)}), bf16[512,2048]{0,1:T(8,128)(2,1)}) %all-gather.8.cloned.1.call-update) | async-done | bytes 2097168 | tf_op jit(solution)/shard_map/all_gather | solution.py:65
  360.4 10.6 %fusion.1 = f32[512,2048]{1,0:T(8,128)} fusion(bf16[512,2048]{0,1:T(8,128)(2,1)} %all-gather.8.cloned.1.call-done, bf16[2048,2048]{1,0:T(8,128)(2,1)} %all-gather.6.cloned.1.call-done), kind=kOutput, calls=%fused_computation.10 | convolution fusion | flops 4294967296 | bytes 14680064 | tf_op jit(solution)/shard_map/dot_general | solution.py:68
  370.9 0.0 copy-start.1
  370.9 0.0 reduce-scatter.2.cloned.1.call-update
  370.9 0.7 copy-done.1
  371.6 3.1 broadcast_in_dim.33
  374.7 10.5 %reshape.42 = pred[512,2048]{1,0:T(8,128)(4,1)S(1)} reshape(pred[16,32,64,32]{3,2,1,0:T(8,128)(4,1)} %broadcast_in_dim.33) | data formatting | bytes 2097152 | tf_op jit(solution)/shard_map/reshape | solution.py:28
  385.2 35.3 %reduce-scatter.2.cloned.1.call-done = f32[512,512]{1,0:T(8,128)} async-done(((f32[512,2048]{1,0:T(8,128)}), f32[512,512]{1,0:T(8,128)}) %reduce-scatter.2.cloned.1.call-update) | async-done | bytes 1048592 | tf_op jit(solution)/shard_map/reduce_scatter | solution.py:69
  420.5 2.3 subtract_convert_fusion
  (2 shorter events, 0.0 us)
Async XLA Ops:
  6.5 57.8 %all-gather.4.cloned.1.call-start = ((), (), s32[]{:S(2)}) async-start(), calls=%async_computation.1 | async-start | bytes 2621440 | tf_op jit(solution)/shard_map/all_gather | solution.py:57
  27.0 95.6 %all-gather.6.cloned.1.call-start = ((), (), s32[]{:S(2)}) async-start(), calls=%async_computation.2 | async-start | bytes 8912896 | tf_op jit(solution)/shard_map/all_gather | solution.py:60
  27.9 332.5 %all-gather.8.cloned.1.call-start = ((), (), s32[]{:S(2)}) async-start(), calls=%async_computation.3 | async-start | bytes 2621440 | tf_op jit(solution)/shard_map/all_gather | solution.py:65
  130.2 97.4 %copy-start = (s32[16,64]{1,0:T(8,128)S(1)}, s32[16,64]{1,0:T(8,128)}, u32[]{:S(2)}) copy-start(s32[16,64]{1,0:T(8,128)} %param.6) | copy-start | bytes 12292
  130.2 92.0 %collective-permute-start = (f32[512,2048]{1,0:T(8,128)S(1)}, f32[512,2048]{1,0:T(8,128)S(1)}, u32[]{:S(2)}, u32[]{:S(2)}) collective-permute-start(f32[512,2048]{1,0:T(8,128)S(1)} %fusion), channel_id=1, source_target_pairs={{0,1},{1,0},{2,3},{3,2},{4,5},{5,4},{6,7},{7,6},{8,9},{9,8},{10,11... | collective-permute-start | bytes 12582920 | tf_op jit(solution)/shard_map/ppermute | solution.py:14
  224.9 92.8 %collective-permute-start.1 = (f32[512,2048]{1,0:T(8,128)}, f32[512,2048]{1,0:T(8,128)}, u32[]{:S(2)}, u32[]{:S(2)}) collective-permute-start(f32[512,2048]{1,0:T(8,128)} %add.20), channel_id=1, source_target_pairs={{0,2},{1,3},{2,0},{3,1},{4,6},{5,7},{6,4},{7,5},{8,10},{9,11},{10,... | collective-permute-start | bytes 12582920 | tf_op jit(solution)/shard_map/ppermute | solution.py:14
  326.9 93.6 %reduce-scatter.2.cloned.1.call-start = ((), (), s32[]{:S(2)}) async-start(), calls=%async_computation.4 | async-start | bytes 5242880 | tf_op jit(solution)/shard_map/reduce_scatter | solution.py:69
  370.9 0.7 copy-start.1
Sparse Core Ops, SparseCore 0:
  27.1 37.2 all-gather.3
  66.2 56.3 all-gather.5
  327.1 33.2 all-gather.7
  371.1 49.3 reduce-scatter.1
